TPU v7x, 128 devices: a whole 4x4x4 slice. The times are simulated.
128 devices in a mesh: dp: 8 (over z, core), mp: 16 (over x, y).
Axes of the slice: x: 4, y: 4, z: 4, core: 2. Of those that a mesh axis runs over, the one named last changes fastest.
Arguments:
- inputs: bfloat16 [3072, 4096], P('dp'), may hold values from -6 to 6
- grad_out: bfloat16 [3072, 22016], P('dp', 'mp'), may hold values from -0.3125 to 0.3125
- error: bfloat16 [8, 4096, 22016], P('dp', None, 'mp'), may hold values from -6 to 6
- q_prev: float32 [22016, 32], P('mp'), may hold values from -6 to 6
Outputs:
- new_error: bfloat16 [8, 4096, 22016], P('dp', None, 'mp')
- q_new: float32 [22016, 32], P('mp')
All inputs are finite; a program needn't handle non-finite values.
Results may differ from a plain program's by a relative error of at most 0.001.
Values sent between devices are 32-bit elements; how exact they have to be, the bound alone decides.
A program may use at most 128 MiB of HBM per device.

v0:
```python
import jax
import jax.numpy as jnp
from jax import lax
from jax.sharding import PartitionSpec as P

ITERS = 2


def local(inputs, grad_out, error, q_prev):
    grad = lax.dot_general(
        inputs, grad_out, (((0,), (0,)), ((), ())), preferred_element_type=jnp.float32
    )
    merged = grad + error[0].astype(jnp.float32)
    replicas = lax.axis_size("dp")
    factor = q_prev
    p_hat = jnp.zeros((merged.shape[0], factor.shape[1]), jnp.float32)
    for step in range(ITERS):
        left = lax.psum(jnp.dot(merged, factor, precision=lax.Precision.HIGHEST), ("dp", "mp"))
        gram = jnp.dot(left.T, left, precision=lax.Precision.HIGHEST)
        lower = jnp.linalg.cholesky(gram)
        p_hat = lax.linalg.triangular_solve(
            lower, left, left_side=False, lower=True, transpose_a=True
        )
        local_q = lax.dot_general(
            merged, p_hat, (((0,), (0,)), ((), ())), precision=lax.Precision.HIGHEST
        )
        factor = lax.psum(local_q, "dp") / replicas
    approx = jnp.dot(p_hat, factor.T, precision=lax.Precision.HIGHEST)
    new_error = (merged - approx).astype(jnp.bfloat16)[None]
    return (new_error, factor)


def solution(mesh):
    placed = (P("dp", None), P("dp", "mp"), P("dp", None, "mp"), P("mp", None))
    return jax.shard_map(
        local,
        mesh=mesh,
        in_specs=placed,
        out_specs=(P("dp", None, "mp"), P("mp", None)),
        check_vma=False,
    )
```

profile of v0, /device:TPU:1, one launch (start us, length us, event | category | flops | bytes accessed | tf_op | source)
XLA Modules:
  0.0 566.0 jit_solution(494324424620760448)
XLA Ops:
  7.2 0.0 all-reduce.5.cloned.1.call-start
  7.2 1.8 copy-done
  9.1 13.5 %convert_add_fusion = f32[4096,1376]{0,1:T(8,128)} fusion(bf16[384,1376]{0,1:T(8,128)(2,1)} %param.8, bf16[384,4096]{1,0:T(8,128)(2,1)S(1)} %copy-done, bf16[1,4096,1376]{1,2,0:T(8,128)(2,1)} %param.9), kind=kOutput, calls=%fused_computation | convolution fusion | flops 4339793920 | bytes 38019072 | tf_op jit(solution)/shard_map/dot_general | solution.py:10
  22.6 19.7 %fusion.13 = f32[4096,32]{0,1:T(8,128)} fusion(f32[4096,1376]{0,1:T(8,128)} %convert_add_fusion, f32[1376,32]{0,1:T(8,128)S(1)} %copy-done.3), kind=kOutput, calls=%fused_computation.27 | convolution fusion | flops 2164260864 | bytes 23244800 | tf_op jit(solution)/shard_map/dot_general | solution.py:18
  42.3 0.0 all-reduce.5.cloned.1.call-update
  42.3 0.2 all-reduce.7.cloned.1.call-start
  42.6 148.4 %all-reduce.5.cloned.1.call-done = f32[4096,32]{0,1:T(8,128)} async-done(((f32[4096,32]{0,1:T(8,128)}), f32[4096,32]{0,1:T(8,128)}) %all-reduce.5.cloned.1.call-update) | async-done | bytes 524304 | tf_op jit(solution)/shard_map/psum | solution.py:18
  191.0 1.8 fusion.14
  192.7 0.1 copy.6
  192.8 2.9 cholesky.44
  195.8 0.6 compare_reduce_fusion.1
  196.4 0.7 fusion.4
  197.1 2.4 custom-call.6
  199.5 1.7 convolution_bitcast_fusion.1
  201.2 22.4 %fusion.15 = f32[1376,32]{0,1:T(8,128)} fusion(f32[4096,1376]{0,1:T(8,128)} %convert_add_fusion, f32[4096,32]{0,1:T(8,128)S(1)} %convolution_bitcast_fusion.1), kind=kOutput, calls=%fused_computation.29 | convolution fusion | flops 2164260864 | bytes 23244800 | tf_op jit(solution)/shard_map/dot_general | solution.py:24
  223.7 0.0 all-reduce.9.cloned.1.call-start
  223.7 56.2 %all-reduce.7.cloned.1.call-done = f32[1376,32]{0,1:T(8,128)} async-done(((f32[1376,32]{0,1:T(8,128)}), f32[1376,32]{0,1:T(8,128)}) %all-reduce.7.cloned.1.call-update) | async-done | bytes 176144 | tf_op jit(solution)/shard_map/psum | solution.py:27
  279.9 17.2 %fusion.1 = f32[4096,32]{0,1:T(8,128)} fusion(f32[4096,1376]{0,1:T(8,128)} %convert_add_fusion, f32[1376,32]{0,1:T(8,128)} %all-reduce.7.cloned.1.call-done), kind=kOutput, calls=%fused_computation.5 | convolution fusion | flops 2164304896 | bytes 23244800 | tf_op jit(solution)/shard_map/dot_general | solution.py:18
  297.1 0.3 all-reduce.11.cloned.1.call-start
  297.4 146.3 %all-reduce.9.cloned.1.call-done = f32[4096,32]{0,1:T(8,128)} async-done(((f32[4096,32]{0,1:T(8,128)}), f32[4096,32]{0,1:T(8,128)}) %all-reduce.9.cloned.1.call-update) | async-done | bytes 524304 | tf_op jit(solution)/shard_map/psum | solution.py:18
  443.7 1.8 fusion.16
  445.4 0.1 copy.7
  445.5 2.9 cholesky.55
  448.5 0.6 compare_reduce_fusion
  449.1 0.7 fusion.5
  449.8 2.4 custom-call.7
  452.2 1.7 convolution_bitcast_fusion
  453.9 0.8 copy-done.1
  454.7 22.4 %fusion.17 = f32[1376,32]{0,1:T(8,128)} fusion(f32[4096,1376]{0,1:T(8,128)} %convert_add_fusion, f32[4096,32]{0,1:T(8,128)S(1)} %convolution_bitcast_fusion), kind=kOutput, calls=%fused_computation.31 | convolution fusion | flops 2164260864 | bytes 23244800 | tf_op jit(solution)/shard_map/dot_general | solution.py:24
  477.2 56.2 %all-reduce.11.cloned.1.call-done = f32[1376,32]{0,1:T(8,128)} async-done(((f32[1376,32]{0,1:T(8,128)}), f32[1376,32]{0,1:T(8,128)}) %all-reduce.11.cloned.1.call-update) | async-done | bytes 176144 | tf_op jit(solution)/shard_map/psum | solution.py:27
  533.4 0.9 broadcast_multiply_fusion
  534.3 25.1 %fusion = bf16[1,4096,1376]{1,2,0:T(8,128)(2,1)} fusion(f32[4096,1376]{0,1:T(8,128)} %convert_add_fusion, f32[4096,32]{0,1:T(8,128)} %copy-done.1, f32[1376,32]{0,1:T(8,128)S(1)} %broadcast_multiply_fusion), kind=kOutput, calls=%fused_computation.2 | convolution fusion | flops 2175533056 | bytes 34516992 | tf_op jit(solution)/shard_map/dot_general | solution.py:28
  (13 shorter events, 0.1 us)
Async XLA Ops:
  7.2 1.9 copy-start
  7.2 15.4 %copy-start.3 = (f32[1376,32]{0,1:T(8,128)S(1)}, f32[1376,32]{0,1:T(8,128)}, u32[]{:S(2)}) copy-start(f32[1376,32]{0,1:T(8,128)} %param.10) | copy-start | bytes 528388
  7.2 183.8 %all-reduce.5.cloned.1.call-start = ((), (), s32[]{:S(2)}) async-start(), calls=%async_computation | async-start | bytes 1048576 | tf_op jit(solution)/shard_map/psum | solution.py:18
  42.3 237.6 %all-reduce.7.cloned.1.call-start = ((), (), s32[]{:S(2)}) async-start(), calls=%async_computation.1 | async-start | bytes 360448 | tf_op jit(solution)/shard_map/psum | solution.py:27
  223.7 220.0 %all-reduce.9.cloned.1.call-start = ((), (), s32[]{:S(2)}) async-start(), calls=%async_computation.2 | async-start | bytes 1048576 | tf_op jit(solution)/shard_map/psum | solution.py:18
  297.1 236.3 %all-reduce.11.cloned.1.call-start = ((), (), s32[]{:S(2)}) async-start(), calls=%async_computation.3 | async-start | bytes 360448 | tf_op jit(solution)/shard_map/psum | solution.py:27
  453.9 0.8 copy-start.1
  534.3 25.1 %copy-start.2 = (f32[1376,32]{0,1:T(8,128)}, f32[1376,32]{0,1:T(8,128)S(1)}, u32[]{:S(2)}) copy-start(f32[1376,32]{0,1:T(8,128)S(1)} %broadcast_multiply_fusion) | copy-start | bytes 528388
Sparse Core Ops, SparseCore 0:
  42.5 148.4 all-reduce.4
  223.8 56.0 all-reduce.6
  297.3 146.3 all-reduce.8
  477.3 56.0 all-reduce.10
where the time goes:
time: 568 us; the launch traced here: 566 us
  waiting for transfers between devices  407 us (72%)
  matrix products  127 us (22%)
  other arithmetic  14.3 us (3%)
  between operations  13.9 us (2%)
    psum x2, waiting for transfers between devices, local(): lax.psum(jnp.dot(merged, factor, precision=lax.Precision.HIGHEST), ('dp',...  295 us
    psum x2, waiting for transfers between devices, local(): factor = lax.psum(local_q, 'dp') / replicas  112 us
    dot_general x2, matrix products, local(): lax.dot_general(merged, p_hat, (((0,), (0,)), ((), ())), precision=lax.Pr...  44.8 us
    dot_general x2, matrix products, local(): jnp.dot(merged, factor, precision=lax.Precision.HIGHEST)  36.9 us
    dot_general x1, matrix products, local(): approx = jnp.dot(p_hat, factor.T, precision=lax.Precision.HIGHEST)  25.1 us
    dot_general x1, matrix products, local(): lax.dot_general(inputs, grad_out, (((0,), (0,)), ((), ())), preferred_ele...  13.5 us
  transfers between devices with their start and end apart: 4, of which 4 were waited for; matrix products, arithmetic and copies ran while one was open for 0% of the time, Pallas kernels for 0%

commit v1 on v0

v1 whole, which is shorter than its diff:
```python
import jax
import jax.numpy as jnp
from jax import lax
from jax.experimental import pallas as pl
from jax.experimental.pallas import tpu as pltpu
from jax.sharding import PartitionSpec as P

MESH = pl.DeviceIdType.MESH
BF, F32 = jnp.bfloat16, jnp.float32
ITERS = 2
UNIT = 512
HALF = 768


def dot(a, b, ca, cb):
    return lax.dot_general(a, b, (((ca,), (cb,)), ((), ())), preferred_element_type=F32)


def exact(a, b, ca, cb):
    return lax.dot_general(
        a, b, (((ca,), (cb,)), ((), ())), precision=lax.Precision.HIGHEST, preferred_element_type=F32
    )


def split(v):
    hi = v.astype(BF)
    rest = v - hi.astype(F32)
    mid = rest.astype(BF)
    low = (rest - mid.astype(F32)).astype(BF)
    return jnp.concatenate([hi, mid, low], axis=0)


def fold(v):
    r = v.shape[0] // 3
    return v[:r] + (v[r : 2 * r] + v[2 * r :])


def inverse_factor(gram):
    r = gram.shape[0]
    row = lax.broadcasted_iota(jnp.int32, (r, 2 * r), 0)
    col = lax.broadcasted_iota(jnp.int32, (r, 2 * r), 1)
    eye = (row == col)[:, :r].astype(F32)
    a = jnp.concatenate([gram, eye], axis=1)
    for j in range(r):
        factor = a[:, j : j + 1] / a[j : j + 1, j : j + 1]
        a = a - jnp.where(row > j, factor, 0.0) * a[j : j + 1, :]
    pivots = jnp.sum(jnp.where(row == col, a, 0.0), axis=1, keepdims=True)
    return a[:, r:] * lax.rsqrt(pivots)


def factors_kernel(
    x_h, y_h, e_h, q0, left_o, right_o, qt_o,
    x, y, e, qs, xq, wacc, sacc, linv,
    pout, pin, pown, slots, pt, wloc, wrx, wz, wfull,
    in_sem, e_sem, cx_s, cx_r, rs_s, rs_r, ag_s, ag_r, fw_s, fw_r, wx_s, wx_r, wz_s, wz_r, wf_s, wf_r,
):
    dp, mp = lax.axis_index("dp"), lax.axis_index("mp")
    z, c = dp // 2, dp % 2
    px, py = mp // 4, mp % 4
    ff = y.shape[0]
    rest = ff - HALF
    partner = (z * 2 + 1 - c, mp)

    def chip(dx, dy, dz):
        return (((z + dz) % 4) * 2 + c, ((px + dx) % 4) * 4 + (py + dy) % 4)

    def far_first(i):
        return (2 + i + i // 2 + 2 * (i // 3)) % 4

    def rows(half, u):
        return pl.ds(pl.multiple_of(half * 2048 + u * UNIT, UNIT), UNIT)

    def remote(src, dst, ss, rs, to):
        return pltpu.make_async_remote_copy(src, dst, ss, rs, device_id=to, device_id_type=MESH)

    def arrived(ref, sem):
        pltpu.make_async_copy(ref, ref, sem).wait()

    barrier = pltpu.get_barrier_semaphore()

    def greet(k, carry):
        pl.semaphore_signal(barrier, inc=1, device_id=chip(k // 16, (k // 4) % 4, k % 4), device_id_type=MESH)
        return carry

    lax.fori_loop(1, 64, greet, 0)
    pl.semaphore_signal(barrier, inc=1, device_id=partner, device_id_type=MESH)

    loads = [
        pltpu.make_async_copy(y_h, y, in_sem.at[0]),
        pltpu.make_async_copy(x_h, x, in_sem.at[1]),
    ]
    for load in loads:
        load.start()

    def e_load(k):
        half = (1 - c) * (1 - k // 4) + c * (k // 4)
        at = rows(half, (px + far_first(k % 4)) % 4)
        return pltpu.make_async_copy(e_h.at[0, :, at], e.at[:, at], e_sem.at[k])

    def start_load(k, carry):
        e_load(k).start()
        return carry

    lax.fori_loop(0, 8, start_load, 0)

    wloc[...] = jnp.zeros_like(wloc)
    qs[...] = split(q0[...])
    loads[0].wait()
    loads[1].wait()
    pl.semaphore_wait(barrier, 64)

    def iteration(it, carry):
        xq[...] = split(fold(dot(qs[...], y[...], 1, 0)))

        def term(half, u):
            at = rows(half, u)
            return fold(dot(qs[...], e[:, at], 1, 0) + dot(xq[...], x[:, at], 1, 0))

        def other_half(i, carry):
            @pl.when(it == 0)
            def _():
                e_load(i).wait()

            u = (px + far_first(i)) % 4
            v = term(1 - c, u)
            for t in range(4):
                pout[it, i, t] = v[:, 128 * t : 128 * t + 128]
            remote(pout.at[it, i], pin.at[it, i], cx_s.at[it], cx_r.at[it, i], partner).start()
            return carry

        lax.fori_loop(0, 4, other_half, 0)

        def own_half(i, carry):
            @pl.when(it == 0)
            def _():
                e_load(i + 4).wait()

            dx = far_first(i)
            u = (px + dx) % 4
            v = term(c, u)
            arrived(pin.at[it, i], cx_r.at[it, i])
            for t in range(4):
                pown[it, u, t] = v[:, 128 * t : 128 * t + 128] + pin[it, i, t]

            def send(j, carry):
                dy, dz = j // 4, j % 4
                src = pown.at[it, u, (py + dy) % 4, pl.ds(pl.multiple_of(((z + dz) % 4) * 8, 8), 8), :]
                remote(src, slots.at[it, dx * 16 + j], rs_s.at[it], rs_r.at[it], chip(dx, dy, dz)).start()
                return carry

            lax.fori_loop(i // 3, 16, send, 0)
            return carry

        lax.fori_loop(0, 4, own_half, 0)

        mine = pl.ds(pl.multiple_of(z * 8, 8), 8)
        slots[it, 0] = pown[it, px, py, mine, :]
        arrived(slots.at[it, pl.ds(1, 63)], rs_r.at[it])
        pt[it, c, px * 4 + py, mine, :] = jnp.sum(slots[it], axis=0)

        def spread(k, carry):
            dx, dy, dz = far_first(k // 16), (k // 4) % 4, k % 4
            tile = pt.at[it, c, px * 4 + py, mine, :]
            remote(tile, tile, ag_s.at[it], ag_r.at[it, dx], chip(dx, dy, dz)).start()
            return carry

        lax.fori_loop(0, 48, spread, 0)
        lax.fori_loop(49, 64, spread, 0)

        wacc[...] = jnp.zeros_like(wacc)
        sacc[...] = jnp.zeros_like(sacc)

        def unit(half, u):
            at = rows(half, u)
            p = split(jnp.concatenate([pt[it, half, u * 4 + t] for t in range(4)], axis=1))
            wacc[...] += dot(p, e[:, at], 1, 1)
            sacc[...] += dot(p, x[:, at], 1, 1)

        def near(i):
            return (px + 4 - far_first(3 - i)) % 4

        def gather(i, carry):
            u = near(i)

            @pl.when(i == 0)
            def _():
                arrived(slots.at[it, pl.ds(0, 15)], ag_r.at[it, 0])

            @pl.when(i > 0)
            def _():
                arrived(slots.at[it, pl.ds(0, 16)], ag_r.at[it, far_first(3 - i)])

            block = pt.at[it, c, pl.ds(u * 4, 4)]
            remote(block, block, fw_s.at[it], fw_r.at[it, i], partner).start()
            unit(c, u)

            @pl.when(i > 0)
            def _():
                v = near(i - 1)
                arrived(pt.at[it, 1 - c, pl.ds(v * 4, 4)], fw_r.at[it, i - 1])
                unit(1 - c, v)

            return carry

        lax.fori_loop(0, 4, gather, 0)
        v = near(3)
        arrived(pt.at[it, 1 - c, pl.ds(v * 4, 4)], fw_r.at[it, 3])
        unit(1 - c, v)

        w = fold(wacc[...] + dot(split(fold(sacc[...])), y[...], 1, 1))
        wloc[it, 0] = w[:, :HALF]
        wloc[it, 1, :, :rest] = w[:, HALF:]
        remote(wloc.at[it, 1 - c], wrx.at[it], wx_s.at[it], wx_r.at[it], partner).start()
        arrived(wrx.at[it], wx_r.at[it])
        wz[it, z] = wloc[it, c] + wrx[it]
        for dz in (2, 1, 3):
            remote(wz.at[it, z], wz.at[it, z], wz_s.at[it], wz_r.at[it, dz], chip(0, 0, dz)).start()

        gram = jnp.zeros((96, 96), F32)

        def add_gram(k, total):
            p = split(jnp.concatenate([pt[it, k // 4, (k % 4) * 4 + t] for t in range(4)], axis=1))
            return total + dot(p, p, 1, 1)

        gram = fold(lax.fori_loop(0, 8, add_gram, gram))
        gram = gram[:, :32] + (gram[:, 32:64] + gram[:, 64:])
        linv[...] = inverse_factor(gram)

        @pl.when(it == ITERS - 1)
        def _():
            def write_left(k, carry):
                p = jnp.concatenate([pt[it, k // 4, (k % 4) * 4 + t] for t in range(4)], axis=1)
                p = split(-exact(linv[...], p, 1, 0))
                left_o[:, rows(0, k)] = jnp.concatenate([p[:32], p[:32], p[32:64], p[32:64]], axis=0)
                return carry

            lax.fori_loop(0, 8, write_left, 0)

        for dz in (1, 3, 2):
            arrived(wz.at[it, (z + 4 - dz) % 4], wz_r.at[it, dz])
        wfull[it, c] = ((wz[it, 0] + wz[it, 1]) + wz[it, 2]) + wz[it, 3]
        remote(wfull.at[it, c], wfull.at[it, c], wf_s.at[it], wf_r.at[it], partner).start()
        arrived(wfull.at[it, 1 - c], wf_r.at[it])
        scale = 0.125 * linv[...]
        first, second = exact(scale, wfull[it, 0], 1, 0), exact(scale, wfull[it, 1], 1, 0)[:, :rest]
        qs[:, :HALF] = split(first)
        qs[:, HALF:] = split(second)

        @pl.when(it == ITERS - 1)
        def _():
            qt_o[:, :HALF] = first
            qt_o[:, HALF:] = second

        arrived(pout.at[it], cx_s.at[it])
        arrived(slots.at[it, pl.ds(1, 63)], rs_s.at[it])
        arrived(slots.at[it, pl.ds(1, 63)], ag_s.at[it])
        arrived(pt.at[it, c], fw_s.at[it])
        arrived(wrx.at[it], wx_s.at[it])
        arrived(wz.at[it, pl.ds(0, 3)], wz_s.at[it])
        arrived(wfull.at[it, c], wf_s.at[it])
        return carry

    lax.fori_loop(0, ITERS, iteration, 0)
    right = qs[:64].astype(F32)
    right_o[...] = jnp.transpose(jnp.concatenate([right, right], axis=0)).astype(BF)


def error_kernel(e, x, left, y, right, qt, out, q_out):
    k = jnp.concatenate([y[...], right[...]], axis=1)
    r = jnp.concatenate([x[...], left[...]], axis=0)
    out[0] = (e[0].astype(F32) + dot(k, r, 1, 0)).astype(BF)

    @pl.when(pl.program_id(0) == 0)
    def _():
        q_out[...] = qt[...]


def local(inputs, grad_out, error, q_prev):
    grad_out, q_prev, error = grad_out.T, q_prev.T, jnp.swapaxes(error, 1, 2)
    tokens, dw = inputs.shape
    rank, ff = q_prev.shape
    vmem = pl.BlockSpec(memory_space=pltpu.VMEM)
    dma = pltpu.SemaphoreType.DMA
    left, right, qt = pl.pallas_call(
        factors_kernel,
        out_shape=(
            jax.ShapeDtypeStruct((4 * rank, dw), BF),
            jax.ShapeDtypeStruct((ff, 4 * rank), BF),
            jax.ShapeDtypeStruct((rank, ff), F32),
        ),
        in_specs=[pl.BlockSpec(memory_space=pl.ANY)] * 3 + [vmem],
        out_specs=(vmem,) * 3,
        scratch_shapes=[
            pltpu.VMEM((tokens, dw), BF),
            pltpu.VMEM((ff, tokens), BF),
            pltpu.VMEM((ff, dw), BF),
            pltpu.VMEM((3 * rank, ff), BF),
            pltpu.VMEM((3 * rank, tokens), BF),
            pltpu.VMEM((3 * rank, ff), F32),
            pltpu.VMEM((3 * rank, tokens), F32),
            pltpu.VMEM((rank, rank), F32),
            pltpu.VMEM((2, 4, 4, rank, 128), F32),
            pltpu.VMEM((2, 4, 4, rank, 128), F32),
            pltpu.VMEM((2, 4, 4, rank, 128), F32),
            pltpu.VMEM((2, 64, 8, 128), F32),
            pltpu.VMEM((2, 2, 16, rank, 128), F32),
            pltpu.VMEM((2, 2, rank, HALF), F32),
            pltpu.VMEM((2, rank, HALF), F32),
            pltpu.VMEM((2, 4, rank, HALF), F32),
            pltpu.VMEM((2, 2, rank, HALF), F32),
            dma((2,)), dma((8,)),
            dma((2,)), dma((2, 4)),
            dma((2,)), dma((2,)),
            dma((2,)), dma((2, 4)),
            dma((2,)), dma((2, 4)),
            dma((2,)), dma((2,)),
            dma((2,)), dma((2, 4)),
            dma((2,)), dma((2,)),
        ],
        compiler_params=pltpu.CompilerParams(
            collective_id=0, has_side_effects=True, vmem_limit_bytes=40 * 2**20
        ),
        name="power_iterations",
    )(inputs, grad_out, error, q_prev)
    step = 512
    new_error, q_new = pl.pallas_call(
        error_kernel,
        grid=(dw // step,),
        out_shape=(jax.ShapeDtypeStruct(error.shape, BF), jax.ShapeDtypeStruct((rank, ff), F32)),
        in_specs=[
            pl.BlockSpec((1, ff, step), lambda i: (0, 0, i)),
            pl.BlockSpec((tokens, step), lambda i: (0, i)),
            pl.BlockSpec((4 * rank, step), lambda i: (0, i)),
            pl.BlockSpec((ff, tokens), lambda i: (0, 0)),
            pl.BlockSpec((ff, 4 * rank), lambda i: (0, 0)),
            pl.BlockSpec((rank, ff), lambda i: (0, 0)),
        ],
        out_specs=(
            pl.BlockSpec((1, ff, step), lambda i: (0, 0, i)),
            pl.BlockSpec((rank, ff), lambda i: (0, 0)),
        ),
        compiler_params=pltpu.CompilerParams(vmem_limit_bytes=32 * 2**20),
        name="new_error",
    )(error, inputs, left, grad_out, right, qt)
    return jnp.swapaxes(new_error, 1, 2), q_new.T


def solution(mesh):
    placed = (P("dp", None), P("dp", "mp"), P("dp", None, "mp"), P("mp", None))
    return jax.shard_map(
        local,
        mesh=mesh,
        in_specs=placed,
        out_specs=(P("dp", None, "mp"), P("mp", None)),
        check_vma=False,
    )
```

time: 568 us -> 95.6 us (0.17)
  waiting for transfers between devices: 407 us -> 0 us
  matrix products: 127 us -> 0 us
  Pallas kernels: 0 us -> 90.1 us
  other arithmetic: 14.3 us -> 0 us
  between operations: 13.9 us -> 0.66 us
    psum x4 -> x0, waiting for transfers between devices: 407 us -> none  [the longest x2 295 us: local(): lax.psum(jnp.dot(merged, factor, precision=lax.Precision.HIGHEST), ('dp',...]
    dot_general x8 -> x0, matrix products: 124 us -> none  [the longest x2 44.8 us: local(): lax.dot_general(merged, p_hat, (((0,), (0,)), ((), ())), precision=lax.Pr...]
    pallas_call x0 -> x2, Pallas kernels: none -> 90.1 us  [the longest x1 80.3 us: local(): pl.pallas_call(factors_kernel, out_shape=(jax.ShapeDtypeStruct((4 * rank,...]
    another operation x10 -> x0, other arithmetic: 13.4 us -> none  [the longest x6 7.19 us: local(): lower = jnp.linalg.cholesky(gram)]
  transfers between devices with their start and end apart: 4 -> 0, of which waited for: 4 -> 0; matrix products, arithmetic and copies ran while one was open for 0% -> 0% of each run, Pallas kernels for 0% -> 0%
where the time goes in v1:
time: 95.6 us; the launch traced here: 95.5 us
  Pallas kernels  90.1 us (94%)
  local copies, waits for them, and re-layouts  4.79 us (5%)
    pallas_call x1, Pallas kernels, local(): pl.pallas_call(factors_kernel, out_shape=(jax.ShapeDtypeStruct((4 * rank,...  80.3 us
    pallas_call x1, Pallas kernels, local(): pl.pallas_call(error_kernel, grid=(dw // step,), out_shape=(jax.ShapeDtyp...  9.73 us
    unnamed x8, local copies, waits for them, and re-layouts  4.79 us

profile of v1, /device:TPU:1, one launch (start us, length us, event | category | flops | bytes accessed | tf_op | source)
XLA Modules:
  0.0 95.5 jit_solution(1638033523489610925)
XLA Ops:
  0.6 0.0 copy-start
  0.6 0.0 copy-start.1
  0.7 2.0 %copy-done.1 = bf16[384,4096]{1,0:T(8,128)(2,1)S(1)} copy-done((bf16[384,4096]{1,0:T(8,128)(2,1)S(1)}, bf16[384,4096]{1,0:T(8,128)(2,1)}, u32[]{:S(2)}) %copy-start.1) | copy-done | bytes 3145752
  2.7 0.0 copy-start.2
  2.7 1.5 %copy-done.2 = bf16[384,1376]{0,1:T(8,128)(2,1)S(1)} copy-done((bf16[384,1376]{0,1:T(8,128)(2,1)S(1)}, bf16[384,1376]{0,1:T(8,128)(2,1)}, u32[]{:S(2)}) %copy-start.2) | copy-done | bytes 1056792
  4.2 0.0 copy-start.3
  4.2 1.3 %copy-done.3 = f32[1376,32]{0,1:T(8,128)S(1)} copy-done((f32[1376,32]{0,1:T(8,128)S(1)}, f32[1376,32]{0,1:T(8,128)}, u32[]{:S(2)}) %copy-start.3) | copy-done | bytes 176152
  5.4 80.3 %power_iterations.1 = (bf16[128,4096]{1,0:T(8,128)(2,1)S(1)}, bf16[1376,128]{1,0:T(8,128)(2,1)S(1)}, f32[32,1376]{1,0:T(8,128)S(1)}) custom-call(bf16[384,4096]{1,0:T(8,128)(2,1)S(1)} %copy-done.1, bf16[1376,384]{1,0:T(8,128)(2,1)S(1)} %bitcast.7, bf16[1,1376,4096]{2,1,0:T(8,128)(2,1)} %bitcast.5, f32[32,1376]{1,0:T(8,128)S(1)} %bitcast.9), custom_call_target="tpu_custom_call" | custom-call | tf_op jit(solution)/shard_map/power_iterations/pallas_call | solution.py:284
  85.8 0.0 copy-done
  85.8 9.7 %new_error.1 = (bf16[1,1376,4096]{2,1,0:T(8,128)(2,1)}, f32[32,1376]{1,0:T(8,128)}) custom-call(bf16[1,1376,4096]{2,1,0:T(8,128)(2,1)S(1)} %bitcast.6, bf16[384,4096]{1,0:T(8,128)(2,1)S(1)} %copy-done.1, bf16[128,4096]{1,0:T(8,128)(2,1)S(1)} %get-tuple-element.7.left, bf16[1376,384]{1,0:T(8,128)(2,1)S(1)} %bitcast.8, ...), custom_call_target="tpu_custom_call" | custom-call | tf_op jit(solution)/shard_map/new_error/pallas_call | solution.py:326
Async XLA Ops:
  0.6 85.1 %copy-start = (bf16[1,4096,1376]{1,2,0:T(8,128)(2,1)S(1)}, bf16[1,4096,1376]{1,2,0:T(8,128)(2,1)}, u32[]{:S(2)}) copy-start(bf16[1,4096,1376]{1,2,0:T(8,128)(2,1)} %param.6) | copy-start | bytes 33816580
  0.6 2.0 %copy-start.1 = (bf16[384,4096]{1,0:T(8,128)(2,1)S(1)}, bf16[384,4096]{1,0:T(8,128)(2,1)}, u32[]{:S(2)}) copy-start(bf16[384,4096]{1,0:T(8,128)(2,1)} %x.1) | copy-start | bytes 9437188
  2.7 1.5 %copy-start.2 = (bf16[384,1376]{0,1:T(8,128)(2,1)S(1)}, bf16[384,1376]{0,1:T(8,128)(2,1)}, u32[]{:S(2)}) copy-start(bf16[384,1376]{0,1:T(8,128)(2,1)} %param.5) | copy-start | bytes 3170308
  4.2 1.3 %copy-start.3 = (f32[1376,32]{0,1:T(8,128)S(1)}, f32[1376,32]{0,1:T(8,128)}, u32[]{:S(2)}) copy-start(f32[1376,32]{0,1:T(8,128)} %param.7) | copy-start | bytes 528388

commit v2 on v0

v2 whole, which is shorter than its diff:
```python
import jax
import jax.numpy as jnp
from jax import lax
from jax.experimental import pallas as pl
from jax.experimental.pallas import tpu as pltpu
from jax.sharding import PartitionSpec as P

MESH = pl.DeviceIdType.MESH
BF, F32 = jnp.bfloat16, jnp.float32
ITERS = 2
UNIT = 512
HALF = 688
DEEP = 1024


def dot(a, b, ca, cb):
    return lax.dot_general(a, b, (((ca,), (cb,)), ((), ())), preferred_element_type=F32)


def exact(a, b, ca, cb):
    return lax.dot_general(
        a, b, (((ca,), (cb,)), ((), ())), precision=lax.Precision.HIGHEST, preferred_element_type=F32
    )


def split(v):
    hi = v.astype(BF)
    rest = v - hi.astype(F32)
    mid = rest.astype(BF)
    low = (rest - mid.astype(F32)).astype(BF)
    return jnp.concatenate([hi, mid, low], axis=0)


def fold(v):
    r = v.shape[0] // 3
    return v[:r] + (v[r : 2 * r] + v[2 * r :])


def inverse_factor(gram):
    r = gram.shape[0]
    row = lax.broadcasted_iota(jnp.int32, (r, 2 * r), 0)
    col = lax.broadcasted_iota(jnp.int32, (r, 2 * r), 1)
    eye = (row == col)[:, :r].astype(F32)
    a = jnp.concatenate([gram, eye], axis=1)
    for j in range(r):
        factor = a[:, j : j + 1] / a[j : j + 1, j : j + 1]
        a = a - jnp.where(row > j, factor, 0.0) * a[j : j + 1, :]
    pivots = jnp.sum(jnp.where(row == col, a, 0.0), axis=1, keepdims=True)
    return a[:, r:] * lax.rsqrt(pivots)


def factors_kernel(
    x_h, y_h, e_h, q0_h, left_o, right_o, qt_o, x, y, e,
    et, q0, qs, ps, xq, pacc, wacc, sacc, linv,
    pout, pin, pown, slots, pt, wloc, wrx, wz, wfull,
    in_sem, near_sem, far_sem, cx_s, cx_r, rs_s, rs_r, ag_s, ag_r, fw_s, fw_r, wx_s, wx_r, wz_s, wz_r, wf_s, wf_r,
):
    dp, mp = lax.axis_index("dp"), lax.axis_index("mp")
    z, c = lax.div(dp, 2), lax.rem(dp, 2)
    px, py = lax.div(mp, 4), lax.rem(mp, 4)
    o = 1 - c
    partner = (z * 2 + o, mp)
    at_x = [lax.rem(px + k, 4) for k in range(4)]
    at_y = [lax.rem(py + k, 4) for k in range(4)]
    at_z = [lax.rem(z + k, 4) for k in range(4)]
    far_first = (2, 1, 3, 0)
    others = [(dx, dy, dz) for dx in far_first for dy in far_first for dz in far_first][:-1]

    def chip(dx, dy, dz):
        return (at_z[dz] * 2 + c, at_x[dx] * 4 + at_y[dy])

    def cols(half, u):
        return pl.ds(pl.multiple_of(half * 2048 + u * UNIT, UNIT), UNIT)

    def deep(k):
        return pl.ds(pl.multiple_of(k * DEEP, DEEP), DEEP)

    def half_rows(h):
        return pl.ds(pl.multiple_of(h * HALF, 16), HALF)

    def remote(src, dst, ss, rs, to):
        return pltpu.make_async_remote_copy(src, dst, ss, rs, device_id=to, device_id_type=MESH)

    def arrived(ref, sem):
        pltpu.make_async_copy(ref, ref, sem).wait()

    barrier = pltpu.get_barrier_semaphore()
    for peer in others:
        pl.semaphore_signal(barrier, inc=1, device_id=chip(*peer), device_id_type=MESH)
    pl.semaphore_signal(barrier, inc=1, device_id=partner, device_id_type=MESH)

    loads = [
        pltpu.make_async_copy(q0_h, q0, in_sem.at[0]),
        pltpu.make_async_copy(y_h, y, in_sem.at[1]),
        pltpu.make_async_copy(x_h, x, in_sem.at[2]),
    ]

    def own_load(k):
        at = (half_rows(c), deep(k))
        return pltpu.make_async_copy(e_h.at[0, at[0], at[1]], e.at[at[0], at[1]], near_sem.at[k])

    def other_load(k):
        at = (half_rows(o), cols(c if k >= 4 else o, at_x[far_first[k % 4]]))
        return pltpu.make_async_copy(e_h.at[0, at[0], at[1]], e.at[at[0], at[1]], far_sem.at[k])

    loads[0].start()
    own_load(0).start()
    loads[1].start()
    for k in range(1, 4):
        own_load(k).start()
    loads[2].start()
    for k in range(8):
        other_load(k).start()

    loads[0].wait()
    for h in range(2):
        qs[h] = split(q0[:, h * HALF : h * HALF + HALF])

    def iteration(it, carry):
        for k in range(4):
            @pl.when(it == 0)
            def _():
                own_load(k).wait()

            pacc[:, deep(k)] = fold(dot(qs[c], e[half_rows(c), deep(k)], 1, 0))

        @pl.when(it > 0)
        def _():
            arrived(wfull.at[it - 1, o], wf_r.at[it - 1])
            qs[o] = split(exact(0.125 * linv[...], wfull[it - 1, o], 1, 0))

        @pl.when(it == 0)
        def _():
            loads[1].wait()
            loads[2].wait()
            pl.semaphore_wait(barrier, 64)

        xq[...] = split(fold(dot(qs[0], y[:HALF], 1, 0) + dot(qs[1], y[HALF:], 1, 0)))

        def term(k, half, u):
            @pl.when(it == 0)
            def _():
                other_load(k).wait()

            at = cols(half, u)
            return pacc[:, at] + fold(dot(qs[o], e[half_rows(o), at], 1, 0) + dot(xq[...], x[:, at], 1, 0))

        for i, dx in enumerate(far_first):
            v = term(i, o, at_x[dx])
            for t in range(4):
                pout[it, i, t] = v[:, 128 * t : 128 * t + 128]
            remote(pout.at[it, i], pin.at[it, i], cx_s.at[it], cx_r.at[it, i], partner).start()

        for i, dx in enumerate(far_first):
            u = at_x[dx]
            v = term(i + 4, c, u)
            arrived(pin.at[it, i], cx_r.at[it, i])
            for t in range(4):
                pown[it, u, t] = v[:, 128 * t : 128 * t + 128] + pin[it, i, t]
            for dy in far_first:
                for dz in far_first:
                    if dx or dy or dz:
                        src = pown.at[it, u, at_y[dy], pl.ds(pl.multiple_of(at_z[dz] * 8, 8), 8), :]
                        slot = slots.at[it, dx * 16 + dy * 4 + dz]
                        remote(src, slot, rs_s.at[it], rs_r.at[it], chip(dx, dy, dz)).start()

        @pl.when(it == 0)
        def _():
            def flip(k, carry):
                for h in range(2):
                    et[h, cols(0, k), :] = jnp.transpose(e[half_rows(h), cols(0, k)])
                return carry

            lax.fori_loop(0, 8, flip, 0)

        mine = pl.ds(pl.multiple_of(z * 8, 8), 8)
        slots[it, 0] = pown[it, px, py, mine, :]
        arrived(slots.at[it, pl.ds(1, 63)], rs_r.at[it])
        pt[it, c, px * 4 + py, mine, :] = jnp.sum(slots[it], axis=0)
        tile = pt.at[it, c, px * 4 + py, mine, :]
        for peer in others:
            remote(tile, tile, ag_s.at[it], ag_r.at[it], chip(*peer)).start()
        arrived(slots.at[it, pl.ds(1, 63)], ag_r.at[it])
        for g in range(2):
            block = pt.at[it, c, pl.ds(8 * g, 8)]
            remote(block, block, fw_s.at[it], fw_r.at[it, g], partner).start()

        def piece(half, g):
            return split(jnp.concatenate([pt[it, half, 8 * g + t] for t in range(8)], axis=1))

        for g in range(2):
            at = deep(2 * c + g)
            p = piece(c, g)
            for h in range(2):
                w = dot(p, et[h, at, :], 1, 0)
                wacc[h] = w if g == 0 else wacc[h] + w
            w = dot(p, x[:, at], 1, 1)
            sacc[...] = w if g == 0 else sacc[...] + w
        for g in range(2):
            arrived(pt.at[it, o, pl.ds(8 * g, 8)], fw_r.at[it, g])
            p = piece(o, g)
            ps[:, g * DEEP : g * DEEP + DEEP] = p
            sacc[...] += dot(p, x[:, deep(2 * o + g)], 1, 1)
        s = split(fold(sacc[...]))

        def finish(h):
            at = pl.ds(pl.multiple_of(o * 2048, 2048), 2048)
            return fold(wacc[h] + dot(ps[...], et[h, at, :], 1, 0) + dot(s, y[half_rows(h), :], 1, 1))

        wloc[it] = finish(o)
        remote(wloc.at[it], wrx.at[it], wx_s.at[it], wx_r.at[it], partner).start()
        w = finish(c)
        arrived(wrx.at[it], wx_r.at[it])
        wz[it, z] = w + wrx[it]
        for dz in (2, 1, 3):
            remote(wz.at[it, z], wz.at[it, z], wz_s.at[it], wz_r.at[it, dz], chip(0, 0, dz)).start()

        def add_gram(k, total):
            p = split(jnp.concatenate([pt[it, k // 2, (k % 2) * 8 + t] for t in range(8)], axis=1))
            return total + dot(p, p, 1, 1)

        gram = fold(lax.fori_loop(0, 4, add_gram, jnp.zeros((96, 96), F32)))
        gram = gram[:, :32] + (gram[:, 32:64] + gram[:, 64:])
        linv[...] = inverse_factor(gram)

        @pl.when(it == ITERS - 1)
        def _():
            def write_left(k, carry):
                p = jnp.concatenate([pt[it, k // 4, (k % 4) * 4 + t] for t in range(4)], axis=1)
                p = split(-exact(linv[...], p, 1, 0))
                left_o[:, cols(0, k)] = jnp.concatenate([p[:32], p[:32], p[32:64], p[32:64]], axis=0)
                return carry

            lax.fori_loop(0, 8, write_left, 0)

        for dz in (1, 3, 2):
            arrived(wz.at[it, at_z[4 - dz]], wz_r.at[it, dz])
        wfull[it, c] = ((wz[it, 0] + wz[it, 1]) + wz[it, 2]) + wz[it, 3]
        remote(wfull.at[it, c], wfull.at[it, c], wf_s.at[it], wf_r.at[it], partner).start()
        qs[c] = split(exact(0.125 * linv[...], wfull[it, c], 1, 0))
        return carry

    lax.fori_loop(0, ITERS, iteration, 0)
    last = ITERS - 1
    arrived(wfull.at[last, o], wf_r.at[last])
    for h in range(2):
        q = exact(0.125 * linv[...], wfull[last, h], 1, 0)
        qt_o[:, h * HALF : h * HALF + HALF] = q
        q = split(q)[:64].astype(F32)
        right_o[h * HALF : h * HALF + HALF] = jnp.transpose(jnp.concatenate([q, q], axis=0)).astype(BF)

    for it in range(ITERS):
        arrived(pout.at[it], cx_s.at[it])
        arrived(slots.at[it, pl.ds(1, 63)], rs_s.at[it])
        arrived(slots.at[it, pl.ds(1, 63)], ag_s.at[it])
        arrived(pt.at[it, c], fw_s.at[it])
        arrived(wrx.at[it], wx_s.at[it])
        arrived(wz.at[it, pl.ds(0, 3)], wz_s.at[it])
        arrived(wfull.at[it, c], wf_s.at[it])


def error_kernel(e, x, left, y, right, qt, out, q_out, stage, sem):
    k = jnp.concatenate([y[...], right[...]], axis=1)
    q_out[...] = qt[...]

    def write(i):
        at = pl.ds(pl.multiple_of(i * DEEP, DEEP), DEEP)
        return pltpu.make_async_copy(stage.at[i % 2], out.at[0, :, at], sem.at[i % 2])

    for i in range(4):
        if i >= 2:
            write(i - 2).wait()
        at = pl.ds(i * DEEP, DEEP)
        r = jnp.concatenate([x[:, at], left[:, at]], axis=0)
        stage[i % 2] = (e[:, at].astype(F32) + dot(k, r, 1, 0)).astype(BF)
        write(i).start()
    write(2).wait()
    write(3).wait()


def local(inputs, grad_out, error, q_prev):
    grad_out, q_prev, error = grad_out.T, q_prev.T, jnp.swapaxes(error, 1, 2)
    tokens, dw = inputs.shape
    rank, ff = q_prev.shape
    vmem = pl.BlockSpec(memory_space=pltpu.VMEM)
    anywhere = pl.BlockSpec(memory_space=pl.ANY)
    dma = pltpu.SemaphoreType.DMA
    left, right, qt, x, y, e = pl.pallas_call(
        factors_kernel,
        out_shape=(
            jax.ShapeDtypeStruct((4 * rank, dw), BF),
            jax.ShapeDtypeStruct((ff, 4 * rank), BF),
            jax.ShapeDtypeStruct((rank, ff), F32),
            jax.ShapeDtypeStruct((tokens, dw), BF),
            jax.ShapeDtypeStruct((ff, tokens), BF),
            jax.ShapeDtypeStruct((ff, dw), BF),
        ),
        in_specs=[anywhere] * 4,
        out_specs=(vmem,) * 6,
        scratch_shapes=[
            pltpu.VMEM((2, dw, HALF), BF),
            pltpu.VMEM((rank, ff), F32),
            pltpu.VMEM((2, 3 * rank, HALF), BF),
            pltpu.VMEM((3 * rank, 2 * DEEP), BF),
            pltpu.VMEM((3 * rank, tokens), BF),
            pltpu.VMEM((rank, dw), F32),
            pltpu.VMEM((2, 3 * rank, HALF), F32),
            pltpu.VMEM((3 * rank, tokens), F32),
            pltpu.VMEM((rank, rank), F32),
            pltpu.VMEM((2, 4, 4, rank, 128), F32),
            pltpu.VMEM((2, 4, 4, rank, 128), F32),
            pltpu.VMEM((2, 4, 4, rank, 128), F32),
            pltpu.VMEM((2, 64, 8, 128), F32),
            pltpu.VMEM((2, 2, 16, rank, 128), F32),
            pltpu.VMEM((2, rank, HALF), F32),
            pltpu.VMEM((2, rank, HALF), F32),
            pltpu.VMEM((2, 4, rank, HALF), F32),
            pltpu.VMEM((2, 2, rank, HALF), F32),
            dma((3,)), dma((4,)), dma((8,)),
            dma((2,)), dma((2, 4)),
            dma((2,)), dma((2,)),
            dma((2,)), dma((2,)),
            dma((2,)), dma((2, 2)),
            dma((2,)), dma((2,)),
            dma((2,)), dma((2, 4)),
            dma((2,)), dma((2,)),
        ],
        compiler_params=pltpu.CompilerParams(
            collective_id=0, has_side_effects=True, vmem_limit_bytes=28 * 2**20
        ),
        name="power_iterations",
    )(*[pltpu.with_memory_space_constraint(v, pltpu.HBM) for v in (inputs, grad_out, error, q_prev)])
    new_error, q_new = pl.pallas_call(
        error_kernel,
        out_shape=(jax.ShapeDtypeStruct(error.shape, BF), jax.ShapeDtypeStruct((rank, ff), F32)),
        in_specs=[vmem] * 6,
        out_specs=(anywhere, vmem),
        scratch_shapes=[pltpu.VMEM((2, ff, DEEP), BF), dma((2,))],
        compiler_params=pltpu.CompilerParams(vmem_limit_bytes=24 * 2**20),
        name="new_error",
    )(e, x, left, y, right, qt)
    return jnp.swapaxes(new_error, 1, 2), q_new.T


def solution(mesh):
    placed = (P("dp", None), P("dp", "mp"), P("dp", None, "mp"), P("mp", None))
    return jax.shard_map(
        local,
        mesh=mesh,
        in_specs=placed,
        out_specs=(P("dp", None, "mp"), P("mp", None)),
        check_vma=False,
    )
```

time: 568 us -> 78.9 us (0.14)
  waiting for transfers between devices: 407 us -> 0 us
  matrix products: 127 us -> 0 us
  Pallas kernels: 0 us -> 78 us
  other arithmetic: 14.3 us -> 0 us
  between operations: 13.9 us -> 0.8 us
    psum x4 -> x0, waiting for transfers between devices: 407 us -> none  [the longest x2 295 us: local(): lax.psum(jnp.dot(merged, factor, precision=lax.Precision.HIGHEST), ('dp',...]
    dot_general x8 -> x0, matrix products: 124 us -> none  [the longest x2 44.8 us: local(): lax.dot_general(merged, p_hat, (((0,), (0,)), ((), ())), precision=lax.Pr...]
    pallas_call x0 -> x2, Pallas kernels: none -> 78 us  [the longest x1 69.3 us: local(): pl.pallas_call(factors_kernel, out_shape=(jax.ShapeDtypeStruct((4 * rank,...]
    another operation x10 -> x0, other arithmetic: 13.4 us -> none  [the longest x6 7.19 us: local(): lower = jnp.linalg.cholesky(gram)]
  transfers between devices with their start and end apart: 4 -> 0, of which waited for: 4 -> 0; matrix products, arithmetic and copies ran while one was open for 0% -> 0% of each run, Pallas kernels for 0% -> 0%
where the time goes in v2:
time: 78.9 us; the launch traced here: 78.8 us
  Pallas kernels  78 us (99%)
  between operations  0.8 us (1%)
    pallas_call x1, Pallas kernels, local(): pl.pallas_call(factors_kernel, out_shape=(jax.ShapeDtypeStruct((4 * rank,...  69.3 us
    pallas_call x1, Pallas kernels, local(): pl.pallas_call(error_kernel, out_shape=(jax.ShapeDtypeStruct(error.shape,...  8.74 us

profile of v2, /device:TPU:1, one launch (start us, length us, event | category | flops | bytes accessed | tf_op | source)
XLA Modules:
  0.0 78.8 jit_solution(6933076058320430100)
XLA Ops:
  0.6 69.3 %power_iterations.1 = (bf16[128,4096]{1,0:T(8,128)(2,1)S(1)}, bf16[1376,128]{1,0:T(8,128)(2,1)S(1)}, f32[32,1376]{1,0:T(8,128)S(1)}, bf16[384,4096]{1,0:T(8,128)...) custom-call(bf16[384,4096]{1,0:T(8,128)(2,1)} %x_h.1, bf16[1376,384]{1,0:T(8,128)(2,1)} %bitcast.6, ...), custom_call_target="tpu_custom_call" | custom-call | tf_op jit(solution)/shard_map/power_iterations/pallas_call | solution.py:288
  69.9 8.7 %new_error.1 = (bf16[1,1376,4096]{2,1,0:T(8,128)(2,1)}, f32[32,1376]{1,0:T(8,128)}) custom-call(bf16[1376,4096]{1,0:T(8,128)(2,1)S(1)} %get-tuple-element.10.e, bf16[384,4096]{1,0:T(8,128)(2,1)S(1)} %get-tuple-element.11.x, bf16[128,4096]{1,0:T(8,128)(2,1)S(1)} %get-tuple-element.12.left, bf16[1376,384]{1,0:T(8,128)(2,1)S(1)} %get-tuple-element.13.y, ...), custom_call_target="tpu_custom_call" | custom-call | tf_op jit(solution)/shard_map/new_error/pallas_call | solution.py:333

commit v3 on v2

--- a/solution.py
+++ b/solution.py
@@ -10,6 +10,7 @@
 ITERS = 2
 UNIT = 512
 HALF = 688
+PARTS = ((0, 256), (256, 256), (512, 176))
 DEEP = 1024
 
 
@@ -50,8 +51,8 @@
 
 
 def factors_kernel(
-    x_h, y_h, e_h, q0_h, left_o, right_o, qt_o, x, y, e,
-    et, q0, qs, ps, xq, pacc, wacc, sacc, linv,
+    x_h, y_h, e_h, q0_h, left_o, right_o, qt_o, base_o,
+    x, y, e, et, q0, qs, ps, xq, tacc, pacc, wacc, sacc, linv,
     pout, pin, pown, slots, pt, wloc, wrx, wz, wfull,
     in_sem, near_sem, far_sem, cx_s, cx_r, rs_s, rs_r, ag_s, ag_r, fw_s, fw_r, wx_s, wx_r, wz_s, wz_r, wf_s, wf_r,
 ):
@@ -78,6 +79,13 @@
     def half_rows(h):
         return pl.ds(pl.multiple_of(h * HALF, 16), HALF)
 
+    def part_rows(h, k):
+        first, width = PARTS[k]
+        return pl.ds(pl.multiple_of(h * HALF + first, 16), width)
+
+    def lanes(k):
+        return pl.ds(*PARTS[k])
+
     def remote(src, dst, ss, rs, to):
         return pltpu.make_async_remote_copy(src, dst, ss, rs, device_id=to, device_id_type=MESH)
 
@@ -96,8 +104,8 @@
     ]
 
     def own_load(k):
-        at = (half_rows(c), deep(k))
-        return pltpu.make_async_copy(e_h.at[0, at[0], at[1]], e.at[at[0], at[1]], near_sem.at[k])
+        at = part_rows(c, k)
+        return pltpu.make_async_copy(e_h.at[0, at, :], e.at[at, :], near_sem.at[k])
 
     def other_load(k):
         at = (half_rows(o), cols(c if k >= 4 else o, at_x[far_first[k % 4]]))
@@ -106,36 +114,42 @@
     loads[0].start()
     own_load(0).start()
     loads[1].start()
-    for k in range(1, 4):
+    for k in range(1, 3):
         own_load(k).start()
     loads[2].start()
     for k in range(8):
         other_load(k).start()
 
+    wz[...] = jnp.zeros_like(wz)
+    wloc[...] = jnp.zeros_like(wloc)
     loads[0].wait()
     for h in range(2):
         qs[h] = split(q0[:, h * HALF : h * HALF + HALF])
 
+    def enter(k):
+        q, at = qs[c, :, lanes(k)], part_rows(c, k)
+        t = dot(q, y[at, :], 1, 0)
+        tacc[...] = t if k == 0 else tacc[...] + t
+        for j in range(2):
+            to = pl.ds(j * 2048, 2048)
+            v = fold(dot(q, e[at, to], 1, 0))
+            pacc[:, to] = v if k == 0 else pacc[:, to] + v
+
+    loads[1].wait()
+    for k in range(3):
+        own_load(k).wait()
+        enter(k)
+    loads[2].wait()
+    pl.semaphore_wait(barrier, 64)
+
     def iteration(it, carry):
-        for k in range(4):
-            @pl.when(it == 0)
-            def _():
-                own_load(k).wait()
-
-            pacc[:, deep(k)] = fold(dot(qs[c], e[half_rows(c), deep(k)], 1, 0))
-
         @pl.when(it > 0)
         def _():
-            arrived(wfull.at[it - 1, o], wf_r.at[it - 1])
-            qs[o] = split(exact(0.125 * linv[...], wfull[it - 1, o], 1, 0))
-
-        @pl.when(it == 0)
-        def _():
-            loads[1].wait()
-            loads[2].wait()
-            pl.semaphore_wait(barrier, 64)
-
-        xq[...] = split(fold(dot(qs[0], y[:HALF], 1, 0) + dot(qs[1], y[HALF:], 1, 0)))
+            for k in range(3):
+                arrived(wfull.at[it - 1, o, k], wf_r.at[it - 1, k])
+                qs[o, :, lanes(k)] = split(exact(0.125 * linv[...], wfull[it - 1, o, k], 1, 0))[:, : PARTS[k][1]]
+
+        xq[...] = split(fold(tacc[...] + dot(qs[o], y[half_rows(o), :], 1, 0)))
 
         def term(k, half, u):
             @pl.when(it == 0)
@@ -180,6 +194,13 @@
         tile = pt.at[it, c, px * 4 + py, mine, :]
         for peer in others:
             remote(tile, tile, ag_s.at[it], ag_r.at[it], chip(*peer)).start()
+
+        def merge(k, carry):
+            at = cols(it, k)
+            base_o[:, at] = dot(y[...], x[:, at], 1, 0) + e[:, at].astype(F32)
+            return carry
+
+        lax.fori_loop(0, 4, merge, 0)
         arrived(slots.at[it, pl.ds(1, 63)], ag_r.at[it])
         for g in range(2):
             block = pt.at[it, c, pl.ds(8 * g, 8)]
@@ -203,17 +224,21 @@
             sacc[...] += dot(p, x[:, deep(2 * o + g)], 1, 1)
         s = split(fold(sacc[...]))
 
-        def finish(h):
+        def finish(h, k):
             at = pl.ds(pl.multiple_of(o * 2048, 2048), 2048)
-            return fold(wacc[h] + dot(ps[...], et[h, at, :], 1, 0) + dot(s, y[half_rows(h), :], 1, 1))
-
-        wloc[it] = finish(o)
-        remote(wloc.at[it], wrx.at[it], wx_s.at[it], wx_r.at[it], partner).start()
-        w = finish(c)
-        arrived(wrx.at[it], wx_r.at[it])
-        wz[it, z] = w + wrx[it]
-        for dz in (2, 1, 3):
-            remote(wz.at[it, z], wz.at[it, z], wz_s.at[it], wz_r.at[it, dz], chip(0, 0, dz)).start()
+            w = wacc[h, :, lanes(k)] + dot(ps[...], et[h, at, lanes(k)], 1, 0)
+            return fold(w + dot(s, y[part_rows(h, k), :], 1, 1))
+
+        for k in range(3):
+            wloc[it, k, :, : PARTS[k][1]] = finish(o, k)
+            remote(wloc.at[it, k], wrx.at[it, k], wx_s.at[it], wx_r.at[it, k], partner).start()
+        for k in range(3):
+            w = finish(c, k)
+            arrived(wrx.at[it, k], wx_r.at[it, k])
+            wz[it, k, z, :, : PARTS[k][1]] = w + wrx[it, k, :, : PARTS[k][1]]
+            mine_z = wz.at[it, k, z]
+            for dz in (2, 1, 3):
+                remote(mine_z, mine_z, wz_s.at[it], wz_r.at[it, k, dz], chip(0, 0, dz)).start()
 
         def add_gram(k, total):
             p = split(jnp.concatenate([pt[it, k // 2, (k % 2) * 8 + t] for t in range(8)], axis=1))
@@ -233,21 +258,33 @@
 
             lax.fori_loop(0, 8, write_left, 0)
 
-        for dz in (1, 3, 2):
-            arrived(wz.at[it, at_z[4 - dz]], wz_r.at[it, dz])
-        wfull[it, c] = ((wz[it, 0] + wz[it, 1]) + wz[it, 2]) + wz[it, 3]
-        remote(wfull.at[it, c], wfull.at[it, c], wf_s.at[it], wf_r.at[it], partner).start()
-        qs[c] = split(exact(0.125 * linv[...], wfull[it, c], 1, 0))
+        for k in range(3):
+            for dz in (1, 3, 2):
+                arrived(wz.at[it, k, at_z[4 - dz]], wz_r.at[it, k, dz])
+            total = ((wz[it, k, 0] + wz[it, k, 1]) + wz[it, k, 2]) + wz[it, k, 3]
+            wfull[it, c, k] = total
+            block = wfull.at[it, c, k]
+            remote(block, block, wf_s.at[it], wf_r.at[it, k], partner).start()
+            qs[c, :, lanes(k)] = split(exact(0.125 * linv[...], total, 1, 0))[:, : PARTS[k][1]]
+
+            @pl.when(it < ITERS - 1)
+            def _():
+                enter(k)
+
         return carry
 
     lax.fori_loop(0, ITERS, iteration, 0)
     last = ITERS - 1
-    arrived(wfull.at[last, o], wf_r.at[last])
+    for k in range(3):
+        arrived(wfull.at[last, o, k], wf_r.at[last, k])
     for h in range(2):
-        q = exact(0.125 * linv[...], wfull[last, h], 1, 0)
-        qt_o[:, h * HALF : h * HALF + HALF] = q
-        q = split(q)[:64].astype(F32)
-        right_o[h * HALF : h * HALF + HALF] = jnp.transpose(jnp.concatenate([q, q], axis=0)).astype(BF)
+        for k in range(3):
+            q = exact(0.125 * linv[...], wfull[last, h, k], 1, 0)
+            first, width = h * HALF + PARTS[k][0], PARTS[k][1]
+            qt_o[:, first : first + width] = q[:, :width]
+            q = split(q)[:64].astype(F32)
+            q = jnp.transpose(jnp.concatenate([q, q], axis=0))
+            right_o[first : first + width] = q[:width].astype(BF)
 
     for it in range(ITERS):
         arrived(pout.at[it], cx_s.at[it])
@@ -255,12 +292,11 @@
         arrived(slots.at[it, pl.ds(1, 63)], ag_s.at[it])
         arrived(pt.at[it, c], fw_s.at[it])
         arrived(wrx.at[it], wx_s.at[it])
-        arrived(wz.at[it, pl.ds(0, 3)], wz_s.at[it])
+        arrived(wz.at[it, pl.ds(0, 3), pl.ds(0, 3)], wz_s.at[it])
         arrived(wfull.at[it, c], wf_s.at[it])
 
 
-def error_kernel(e, x, left, y, right, qt, out, q_out, stage, sem):
-    k = jnp.concatenate([y[...], right[...]], axis=1)
+def error_kernel(base, left, right, qt, out, q_out, stage, sem):
     q_out[...] = qt[...]
 
     def write(i):
@@ -271,8 +307,7 @@
         if i >= 2:
             write(i - 2).wait()
         at = pl.ds(i * DEEP, DEEP)
-        r = jnp.concatenate([x[:, at], left[:, at]], axis=0)
-        stage[i % 2] = (e[:, at].astype(F32) + dot(k, r, 1, 0)).astype(BF)
+        stage[i % 2] = (base[:, at] + dot(right[...], left[:, at], 1, 0)).astype(BF)
         write(i).start()
     write(2).wait()
     write(3).wait()
@@ -285,24 +320,26 @@
     vmem = pl.BlockSpec(memory_space=pltpu.VMEM)
     anywhere = pl.BlockSpec(memory_space=pl.ANY)
     dma = pltpu.SemaphoreType.DMA
-    left, right, qt, x, y, e = pl.pallas_call(
+    left, right, qt, base = pl.pallas_call(
         factors_kernel,
         out_shape=(
-            jax.ShapeDtypeStruct((4 * rank, dw), BF),
-            jax.ShapeDtypeStruct((ff, 4 * rank), BF),
-            jax.ShapeDtypeStruct((rank, ff), F32),
-            jax.ShapeDtypeStruct((tokens, dw), BF),
-            jax.ShapeDtypeStruct((ff, tokens), BF),
-            jax.ShapeDtypeStruct((ff, dw), BF),
+            pltpu.VMEM((4 * rank, dw), BF),
+            pltpu.VMEM((ff, 4 * rank), BF),
+            pltpu.VMEM((rank, ff), F32),
+            pltpu.VMEM((ff, dw), F32),
         ),
         in_specs=[anywhere] * 4,
-        out_specs=(vmem,) * 6,
+        out_specs=(vmem,) * 4,
         scratch_shapes=[
+            pltpu.VMEM((tokens, dw), BF),
+            pltpu.VMEM((ff, tokens), BF),
+            pltpu.VMEM((ff, dw), BF),
             pltpu.VMEM((2, dw, HALF), BF),
             pltpu.VMEM((rank, ff), F32),
             pltpu.VMEM((2, 3 * rank, HALF), BF),
             pltpu.VMEM((3 * rank, 2 * DEEP), BF),
             pltpu.VMEM((3 * rank, tokens), BF),
+            pltpu.VMEM((3 * rank, tokens), F32),
             pltpu.VMEM((rank, dw), F32),
             pltpu.VMEM((2, 3 * rank, HALF), F32),
             pltpu.VMEM((3 * rank, tokens), F32),
@@ -312,33 +349,33 @@
             pltpu.VMEM((2, 4, 4, rank, 128), F32),
             pltpu.VMEM((2, 64, 8, 128), F32),
             pltpu.VMEM((2, 2, 16, rank, 128), F32),
-            pltpu.VMEM((2, rank, HALF), F32),
-            pltpu.VMEM((2, rank, HALF), F32),
-            pltpu.VMEM((2, 4, rank, HALF), F32),
-            pltpu.VMEM((2, 2, rank, HALF), F32),
-            dma((3,)), dma((4,)), dma((8,)),
+            pltpu.VMEM((2, 3, rank, 256), F32),
+            pltpu.VMEM((2, 3, rank, 256), F32),
+            pltpu.VMEM((2, 3, 4, rank, 256), F32),
+            pltpu.VMEM((2, 2, 3, rank, 256), F32),
+            dma((3,)), dma((3,)), dma((8,)),
             dma((2,)), dma((2, 4)),
             dma((2,)), dma((2,)),
             dma((2,)), dma((2,)),
             dma((2,)), dma((2, 2)),
-            dma((2,)), dma((2,)),
-            dma((2,)), dma((2, 4)),
-            dma((2,)), dma((2,)),
+            dma((2,)), dma((2, 3)),
+            dma((2,)), dma((2, 3, 4)),
+            dma((2,)), dma((2, 3)),
         ],
         compiler_params=pltpu.CompilerParams(
-            collective_id=0, has_side_effects=True, vmem_limit_bytes=28 * 2**20
+            collective_id=0, has_side_effects=True, vmem_limit_bytes=36 * 2**20
         ),
         name="power_iterations",
     )(*[pltpu.with_memory_space_constraint(v, pltpu.HBM) for v in (inputs, grad_out, error, q_prev)])
     new_error, q_new = pl.pallas_call(
         error_kernel,
         out_shape=(jax.ShapeDtypeStruct(error.shape, BF), jax.ShapeDtypeStruct((rank, ff), F32)),
-        in_specs=[vmem] * 6,
+        in_specs=[vmem] * 4,
         out_specs=(anywhere, vmem),
         scratch_shapes=[pltpu.VMEM((2, ff, DEEP), BF), dma((2,))],
-        compiler_params=pltpu.CompilerParams(vmem_limit_bytes=24 * 2**20),
+        compiler_params=pltpu.CompilerParams(vmem_limit_bytes=16 * 2**20),
         name="new_error",
-    )(e, x, left, y, right, qt)
+    )(base, left, right, qt)
     return jnp.swapaxes(new_error, 1, 2), q_new.T
 
 

time: 78.9 us -> 75.8 us (0.961)
  Pallas kernels: 78 us -> 75 us
    pallas_call x1, Pallas kernels: 8.74 us -> 6.52 us  [local(): pl.pallas_call(error_kernel, out_shape=(jax.ShapeDtypeStruct(error.shape,...]
where the time goes in v3:
time: 75.8 us; the launch traced here: 75.7 us
  Pallas kernels  75 us (99%)
    pallas_call x1, Pallas kernels, local(): pl.pallas_call(factors_kernel, out_shape=(pltpu.VMEM((4 * rank, dw), BF),...  68.5 us
    pallas_call x1, Pallas kernels, local(): pl.pallas_call(error_kernel, out_shape=(jax.ShapeDtypeStruct(error.shape,...  6.52 us

profile of v3, /device:TPU:1, one launch (start us, length us, event | category | flops | bytes accessed | tf_op | source)
XLA Modules:
  0.0 75.7 jit_solution(11244651110801857856)
XLA Ops:
  0.6 68.5 %power_iterations.1 = (bf16[128,4096]{1,0:T(8,128)(2,1)S(1)}, bf16[1376,128]{1,0:T(8,128)(2,1)S(1)}, f32[32,1376]{1,0:T(8,128)S(1)}, f32[1376,4096]{1,0:T(8,128)S(1)}) custom-call(bf16[384,4096]{1,0:T(8,128)(2,1)} %x_h.1, bf16[1376,384]{1,0:T(8,128)(2,1)} %bitcast.6, bf16[1,1376,4096]{2,1,0:T(8,128)(2,1)} %bitcast.5, f32[32,1376]{1,0:T(8,128)} %bitcast.7), custom_call_target="tpu_custom_call" | custom-call | tf_op jit(solution)/shard_map/power_iterations/pallas_call | solution.py:323
  69.1 6.5 %new_error.1 = (bf16[1,1376,4096]{2,1,0:T(8,128)(2,1)}, f32[32,1376]{1,0:T(8,128)}) custom-call(f32[1376,4096]{1,0:T(8,128)S(1)} %get-tuple-element.8.base, bf16[128,4096]{1,0:T(8,128)(2,1)S(1)} %get-tuple-element.9.left, bf16[1376,128]{1,0:T(8,128)(2,1)S(1)} %get-tuple-element.10.right, f32[32,1376]{1,0:T(8,128)S(1)} %get-tuple-element.11.qt), custom_call_target="tpu_custom_call" | custom-call | tf_op jit(solution)/shard_map/new_error/pallas_call | solution.py:370

commit v4 on v3

--- a/solution.py
+++ b/solution.py
@@ -54,7 +54,7 @@
     x_h, y_h, e_h, q0_h, left_o, right_o, qt_o, base_o,
     x, y, e, et, q0, qs, ps, xq, tacc, pacc, wacc, sacc, linv,
     pout, pin, pown, slots, pt, wloc, wrx, wz, wfull,
-    in_sem, near_sem, far_sem, cx_s, cx_r, rs_s, rs_r, ag_s, ag_r, fw_s, fw_r, wx_s, wx_r, wz_s, wz_r, wf_s, wf_r,
+    in_sem, e_sem, cx_s, cx_r, rs_s, rs_r, ag_s, ag_r, fw_s, fw_r, wx_s, wx_r, wz_s, wz_r, wf_s, wf_r,
 ):
     dp, mp = lax.axis_index("dp"), lax.axis_index("mp")
     z, c = lax.div(dp, 2), lax.rem(dp, 2)
@@ -65,7 +65,11 @@
     at_y = [lax.rem(py + k, 4) for k in range(4)]
     at_z = [lax.rem(z + k, 4) for k in range(4)]
     far_first = (2, 1, 3, 0)
+    odd = lax.rem(px, 2)
+    pairs = (lax.div(at_x[2], 2), 1 - lax.div(at_x[2], 2))
+    pair_offsets = ((2, 3 - 2 * odd), (1 + 2 * odd, 0))
     others = [(dx, dy, dz) for dx in far_first for dy in far_first for dz in far_first][:-1]
+    others.sort(key=lambda peer: -sum(min(k, 4 - k) for k in peer))
 
     def chip(dx, dy, dz):
         return (at_z[dz] * 2 + c, at_x[dx] * 4 + at_y[dy])
@@ -103,22 +107,19 @@
         pltpu.make_async_copy(x_h, x, in_sem.at[2]),
     ]
 
-    def own_load(k):
-        at = part_rows(c, k)
-        return pltpu.make_async_copy(e_h.at[0, at, :], e.at[at, :], near_sem.at[k])
-
-    def other_load(k):
-        at = (half_rows(o), cols(c if k >= 4 else o, at_x[far_first[k % 4]]))
-        return pltpu.make_async_copy(e_h.at[0, at[0], at[1]], e.at[at[0], at[1]], far_sem.at[k])
+    order = ((c, 0), (c, 1), (c, 2), (o, 0), (o, 1), (o, 2))
+
+    def part_load(n):
+        at = part_rows(*order[n])
+        return pltpu.make_async_copy(e_h.at[0, at, :], e.at[at, :], e_sem.at[n])
 
     loads[0].start()
-    own_load(0).start()
+    part_load(0).start()
     loads[1].start()
-    for k in range(1, 3):
-        own_load(k).start()
+    for n in range(1, 5):
+        part_load(n).start()
     loads[2].start()
-    for k in range(8):
-        other_load(k).start()
+    part_load(5).start()
 
     wz[...] = jnp.zeros_like(wz)
     wloc[...] = jnp.zeros_like(wloc)
@@ -126,69 +127,74 @@
     for h in range(2):
         qs[h] = split(q0[:, h * HALF : h * HALF + HALF])
 
-    def enter(k):
-        q, at = qs[c, :, lanes(k)], part_rows(c, k)
+    def enter(h, k, first=False):
+        q, at = qs[h, :, lanes(k)], part_rows(h, k)
         t = dot(q, y[at, :], 1, 0)
-        tacc[...] = t if k == 0 else tacc[...] + t
+        tacc[...] = t if first else tacc[...] + t
         for j in range(2):
             to = pl.ds(j * 2048, 2048)
             v = fold(dot(q, e[at, to], 1, 0))
-            pacc[:, to] = v if k == 0 else pacc[:, to] + v
+            pacc[:, to] = v if first else pacc[:, to] + v
+
+    def take(it, h, k):
+        qs[h, :, lanes(k)] = split(exact(0.125 * linv[...], wfull[it, h, k], 1, 0))[:, : PARTS[k][1]]
+
+    def take_partner(it, k):
+        arrived(wfull.at[it, o, k], wf_r.at[it, k])
+        take(it, o, k)
 
     loads[1].wait()
-    for k in range(3):
-        own_load(k).wait()
-        enter(k)
+    for n in range(5):
+        part_load(n).wait()
+        enter(*order[n], first=n == 0)
     loads[2].wait()
+    part_load(5).wait()
     pl.semaphore_wait(barrier, 64)
 
     def iteration(it, carry):
         @pl.when(it > 0)
         def _():
-            for k in range(3):
-                arrived(wfull.at[it - 1, o, k], wf_r.at[it - 1, k])
-                qs[o, :, lanes(k)] = split(exact(0.125 * linv[...], wfull[it - 1, o, k], 1, 0))[:, : PARTS[k][1]]
-
-        xq[...] = split(fold(tacc[...] + dot(qs[o], y[half_rows(o), :], 1, 0)))
-
-        def term(k, half, u):
-            @pl.when(it == 0)
-            def _():
-                other_load(k).wait()
-
-            at = cols(half, u)
-            return pacc[:, at] + fold(dot(qs[o], e[half_rows(o), at], 1, 0) + dot(xq[...], x[:, at], 1, 0))
-
-        for i, dx in enumerate(far_first):
-            v = term(i, o, at_x[dx])
-            for t in range(4):
-                pout[it, i, t] = v[:, 128 * t : 128 * t + 128]
+            take_partner(it - 1, 2)
+
+        q, last_rows = qs[o, :, lanes(2)], part_rows(o, 2)
+        xq[...] = split(fold(tacc[...] + dot(q, y[last_rows, :], 1, 0)))
+
+        def term(half, pair):
+            at = deep(half * 2 + pair)
+            v = pacc[:, at] + fold(dot(qs[o, :, lanes(2)], e[last_rows, at], 1, 0) + dot(xq[...], x[:, at], 1, 0))
+            return [v[:, 128 * t : 128 * t + 128] for t in range(8)]
+
+        for i in range(2):
+            for t, v in enumerate(term(o, pairs[i])):
+                pout[it, i, t] = v
             remote(pout.at[it, i], pin.at[it, i], cx_s.at[it], cx_r.at[it, i], partner).start()
 
-        for i, dx in enumerate(far_first):
-            u = at_x[dx]
-            v = term(i + 4, c, u)
+        for i in range(2):
+            parts = term(c, pairs[i])
             arrived(pin.at[it, i], cx_r.at[it, i])
-            for t in range(4):
-                pown[it, u, t] = v[:, 128 * t : 128 * t + 128] + pin[it, i, t]
-            for dy in far_first:
-                for dz in far_first:
-                    if dx or dy or dz:
-                        src = pown.at[it, u, at_y[dy], pl.ds(pl.multiple_of(at_z[dz] * 8, 8), 8), :]
-                        slot = slots.at[it, dx * 16 + dy * 4 + dz]
-                        remote(src, slot, rs_s.at[it], rs_r.at[it], chip(dx, dy, dz)).start()
+            for t, v in enumerate(parts):
+                pown[it, pairs[i] * 8 + t] = v + pin[it, i, t]
+            for dx in pair_offsets[i]:
+                to_x = lax.rem(px + dx, 4)
+                for dy in far_first:
+                    for dz in far_first:
+                        if i == 0 or dy or dz or dx is not pair_offsets[1][1]:
+                            src = pown.at[it, to_x * 4 + at_y[dy], pl.ds(pl.multiple_of(at_z[dz] * 8, 8), 8), :]
+                            slot = slots.at[it, dx * 16 + dy * 4 + dz]
+                            to = (at_z[dz] * 2 + c, to_x * 4 + at_y[dy])
+                            remote(src, slot, rs_s.at[it], rs_r.at[it], to).start()
+
+        def flip(k, carry):
+            for h in range(2):
+                et[h, cols(0, k), :] = jnp.transpose(e[half_rows(h), cols(0, k)])
+            return carry
 
         @pl.when(it == 0)
         def _():
-            def flip(k, carry):
-                for h in range(2):
-                    et[h, cols(0, k), :] = jnp.transpose(e[half_rows(h), cols(0, k)])
-                return carry
-
-            lax.fori_loop(0, 8, flip, 0)
+            lax.fori_loop(0, 6, flip, 0)
 
         mine = pl.ds(pl.multiple_of(z * 8, 8), 8)
-        slots[it, 0] = pown[it, px, py, mine, :]
+        slots[it, 0] = pown[it, px * 4 + py, mine, :]
         arrived(slots.at[it, pl.ds(1, 63)], rs_r.at[it])
         pt[it, c, px * 4 + py, mine, :] = jnp.sum(slots[it], axis=0)
         tile = pt.at[it, c, px * 4 + py, mine, :]
@@ -201,6 +207,11 @@
             return carry
 
         lax.fori_loop(0, 4, merge, 0)
+
+        @pl.when(it == 0)
+        def _():
+            lax.fori_loop(6, 8, flip, 0)
+
         arrived(slots.at[it, pl.ds(1, 63)], ag_r.at[it])
         for g in range(2):
             block = pt.at[it, c, pl.ds(8 * g, 8)]
@@ -265,26 +276,33 @@
             wfull[it, c, k] = total
             block = wfull.at[it, c, k]
             remote(block, block, wf_s.at[it], wf_r.at[it, k], partner).start()
-            qs[c, :, lanes(k)] = split(exact(0.125 * linv[...], total, 1, 0))[:, : PARTS[k][1]]
+            take(it, c, k)
 
             @pl.when(it < ITERS - 1)
             def _():
-                enter(k)
+                enter(c, k, first=k == 0)
+                if k > 0:
+                    take_partner(it, k - 1)
+                    enter(o, k - 1)
 
         return carry
 
     lax.fori_loop(0, ITERS, iteration, 0)
     last = ITERS - 1
+
+    def lay_out(h, k):
+        q = qs[h, :64, lanes(k)].astype(F32)
+        right_o[part_rows(h, k)] = jnp.transpose(jnp.concatenate([q, q], axis=0)).astype(BF)
+
     for k in range(3):
-        arrived(wfull.at[last, o, k], wf_r.at[last, k])
+        lay_out(c, k)
+    for k in range(3):
+        take_partner(last, k)
+        lay_out(o, k)
     for h in range(2):
         for k in range(3):
-            q = exact(0.125 * linv[...], wfull[last, h, k], 1, 0)
             first, width = h * HALF + PARTS[k][0], PARTS[k][1]
-            qt_o[:, first : first + width] = q[:, :width]
-            q = split(q)[:64].astype(F32)
-            q = jnp.transpose(jnp.concatenate([q, q], axis=0))
-            right_o[first : first + width] = q[:width].astype(BF)
+            qt_o[:, first : first + width] = exact(0.125 * linv[...], wfull[last, h, k], 1, 0)[:, :width]
 
     for it in range(ITERS):
         arrived(pout.at[it], cx_s.at[it])
@@ -296,21 +314,17 @@
         arrived(wfull.at[it, c], wf_s.at[it])
 
 
-def error_kernel(base, left, right, qt, out, q_out, stage, sem):
+def error_kernel(base, left, right, qt, out, q_out, wide, narrow, sem):
+    blocks = ((0, 2048, wide), (2048, 1024, narrow.at[0]), (3072, 1024, narrow.at[1]))
+    writes = []
+    for i, (first, width, stage) in enumerate(blocks):
+        at = pl.ds(first, width)
+        stage[...] = (base[:, at] + dot(right[...], left[:, at], 1, 0)).astype(BF)
+        writes.append(pltpu.make_async_copy(stage, out.at[0, :, at], sem.at[i]))
+        writes[i].start()
     q_out[...] = qt[...]
-
-    def write(i):
-        at = pl.ds(pl.multiple_of(i * DEEP, DEEP), DEEP)
-        return pltpu.make_async_copy(stage.at[i % 2], out.at[0, :, at], sem.at[i % 2])
-
-    for i in range(4):
-        if i >= 2:
-            write(i - 2).wait()
-        at = pl.ds(i * DEEP, DEEP)
-        stage[i % 2] = (base[:, at] + dot(right[...], left[:, at], 1, 0)).astype(BF)
-        write(i).start()
-    write(2).wait()
-    write(3).wait()
+    for write in writes:
+        write.wait()
 
 
 def local(inputs, grad_out, error, q_prev):
@@ -344,17 +358,17 @@
             pltpu.VMEM((2, 3 * rank, HALF), F32),
             pltpu.VMEM((3 * rank, tokens), F32),
             pltpu.VMEM((rank, rank), F32),
-            pltpu.VMEM((2, 4, 4, rank, 128), F32),
-            pltpu.VMEM((2, 4, 4, rank, 128), F32),
-            pltpu.VMEM((2, 4, 4, rank, 128), F32),
+            pltpu.VMEM((2, 2, 8, rank, 128), F32),
+            pltpu.VMEM((2, 2, 8, rank, 128), F32),
+            pltpu.VMEM((2, 16, rank, 128), F32),
             pltpu.VMEM((2, 64, 8, 128), F32),
             pltpu.VMEM((2, 2, 16, rank, 128), F32),
             pltpu.VMEM((2, 3, rank, 256), F32),
             pltpu.VMEM((2, 3, rank, 256), F32),
             pltpu.VMEM((2, 3, 4, rank, 256), F32),
             pltpu.VMEM((2, 2, 3, rank, 256), F32),
-            dma((3,)), dma((3,)), dma((8,)),
-            dma((2,)), dma((2, 4)),
+            dma((3,)), dma((6,)),
+            dma((2,)), dma((2, 2)),
             dma((2,)), dma((2,)),
             dma((2,)), dma((2,)),
             dma((2,)), dma((2, 2)),
@@ -372,8 +386,8 @@
         out_shape=(jax.ShapeDtypeStruct(error.shape, BF), jax.ShapeDtypeStruct((rank, ff), F32)),
         in_specs=[vmem] * 4,
         out_specs=(anywhere, vmem),
-        scratch_shapes=[pltpu.VMEM((2, ff, DEEP), BF), dma((2,))],
-        compiler_params=pltpu.CompilerParams(vmem_limit_bytes=16 * 2**20),
+        scratch_shapes=[pltpu.VMEM((ff, 2 * DEEP), BF), pltpu.VMEM((2, ff, DEEP), BF), dma((3,))],
+        compiler_params=pltpu.CompilerParams(vmem_limit_bytes=24 * 2**20),
         name="new_error",
     )(base, left, right, qt)
     return jnp.swapaxes(new_error, 1, 2), q_new.T

time: 75.8 us -> 75.3 us (level)
  no operation moved by 1% of the time
where the time goes in v4:
time: 75.3 us; the launch traced here: 75.2 us
  Pallas kernels  74.6 us (99%)
    pallas_call x1, Pallas kernels, local(): pl.pallas_call(factors_kernel, out_shape=(pltpu.VMEM((4 * rank, dw), BF),...  68 us
    pallas_call x1, Pallas kernels, local(): pl.pallas_call(error_kernel, out_shape=(jax.ShapeDtypeStruct(error.shape,...  6.59 us

profile of v4, /device:TPU:1, one launch (start us, length us, event | category | flops | bytes accessed | tf_op | source)
XLA Modules:
  0.0 75.2 jit_solution(3222320073173469660)
XLA Ops:
  0.6 68.0 %power_iterations.1 = (bf16[128,4096]{1,0:T(8,128)(2,1)S(1)}, bf16[1376,128]{1,0:T(8,128)(2,1)S(1)}, f32[32,1376]{1,0:T(8,128)S(1)}, f32[1376,4096]{1,0:T(8,128)S(1)}) custom-call(bf16[384,4096]{1,0:T(8,128)(2,1)} %x_h.1, bf16[1376,384]{1,0:T(8,128)(2,1)} %bitcast.6, bf16[1,1376,4096]{2,1,0:T(8,128)(2,1)} %bitcast.5, f32[32,1376]{1,0:T(8,128)} %bitcast.7), custom_call_target="tpu_custom_call" | custom-call | tf_op jit(solution)/shard_map/power_iterations/pallas_call | solution.py:337
  68.6 6.6 %new_error.1 = (bf16[1,1376,4096]{2,1,0:T(8,128)(2,1)}, f32[32,1376]{1,0:T(8,128)}) custom-call(f32[1376,4096]{1,0:T(8,128)S(1)} %get-tuple-element.8.base, bf16[128,4096]{1,0:T(8,128)(2,1)S(1)} %get-tuple-element.9.left, bf16[1376,128]{1,0:T(8,128)(2,1)S(1)} %get-tuple-element.10.right, f32[32,1376]{1,0:T(8,128)S(1)} %get-tuple-element.11.qt), custom_call_target="tpu_custom_call" | custom-call | tf_op jit(solution)/shard_map/new_error/pallas_call | solution.py:384

commit v5 on v4

--- a/solution.py
+++ b/solution.py
@@ -314,14 +314,16 @@
         arrived(wfull.at[it, c], wf_s.at[it])
 
 
-def error_kernel(base, left, right, qt, out, q_out, wide, narrow, sem):
-    blocks = ((0, 2048, wide), (2048, 1024, narrow.at[0]), (3072, 1024, narrow.at[1]))
+def error_kernel(base, left, right, qt, out, q_out, stage, sem):
     writes = []
-    for i, (first, width, stage) in enumerate(blocks):
-        at = pl.ds(first, width)
-        stage[...] = (base[:, at] + dot(right[...], left[:, at], 1, 0)).astype(BF)
-        writes.append(pltpu.make_async_copy(stage, out.at[0, :, at], sem.at[i]))
-        writes[i].start()
+    for first in range(0, 4096, DEEP):
+        at = pl.ds(first, DEEP)
+        stage[:, at] = (base[:, at] + dot(right[...], left[:, at], 1, 0)).astype(BF)
+        for k in range(4):
+            piece = pl.ds(first + k * 256, 256)
+            write = pltpu.make_async_copy(stage.at[:, piece], out.at[0, :, piece], sem.at[len(writes)])
+            write.start()
+            writes.append(write)
     q_out[...] = qt[...]
     for write in writes:
         write.wait()
@@ -386,7 +388,7 @@
         out_shape=(jax.ShapeDtypeStruct(error.shape, BF), jax.ShapeDtypeStruct((rank, ff), F32)),
         in_specs=[vmem] * 4,
         out_specs=(anywhere, vmem),
-        scratch_shapes=[pltpu.VMEM((ff, 2 * DEEP), BF), pltpu.VMEM((2, ff, DEEP), BF), dma((3,))],
+        scratch_shapes=[pltpu.VMEM((ff, dw), BF), dma((16,))],
         compiler_params=pltpu.CompilerParams(vmem_limit_bytes=24 * 2**20),
         name="new_error",
     )(base, left, right, qt)

time: 75.3 us -> 74.6 us (level)
  Pallas kernels: 74.6 us -> 73.8 us
where the time goes in v5:
time: 74.6 us; the launch traced here: 74.5 us
  Pallas kernels  73.8 us (99%)
    pallas_call x1, Pallas kernels, local(): pl.pallas_call(factors_kernel, out_shape=(pltpu.VMEM((4 * rank, dw), BF),...  68 us
    pallas_call x1, Pallas kernels, local(): pl.pallas_call(error_kernel, out_shape=(jax.ShapeDtypeStruct(error.shape,...  5.86 us

profile of v5, /device:TPU:1, one launch (start us, length us, event | category | flops | bytes accessed | tf_op | source)
XLA Modules:
  0.0 74.5 jit_solution(7145466820516375197)
XLA Ops:
  0.6 68.0 %power_iterations.1 = (bf16[128,4096]{1,0:T(8,128)(2,1)S(1)}, bf16[1376,128]{1,0:T(8,128)(2,1)S(1)}, f32[32,1376]{1,0:T(8,128)S(1)}, f32[1376,4096]{1,0:T(8,128)S(1)}) custom-call(bf16[384,4096]{1,0:T(8,128)(2,1)} %x_h.1, bf16[1376,384]{1,0:T(8,128)(2,1)} %bitcast.6, bf16[1,1376,4096]{2,1,0:T(8,128)(2,1)} %bitcast.5, f32[32,1376]{1,0:T(8,128)} %bitcast.7), custom_call_target="tpu_custom_call" | custom-call | tf_op jit(solution)/shard_map/power_iterations/pallas_call | solution.py:339
  68.6 5.9 %new_error.1 = (bf16[1,1376,4096]{2,1,0:T(8,128)(2,1)}, f32[32,1376]{1,0:T(8,128)}) custom-call(f32[1376,4096]{1,0:T(8,128)S(1)} %get-tuple-element.8.base, bf16[128,4096]{1,0:T(8,128)(2,1)S(1)} %get-tuple-element.9.left, bf16[1376,128]{1,0:T(8,128)(2,1)S(1)} %get-tuple-element.10.right, f32[32,1376]{1,0:T(8,128)S(1)} %get-tuple-element.11.qt), custom_call_target="tpu_custom_call" | custom-call | tf_op jit(solution)/shard_map/new_error/pallas_call | solution.py:386

commit v6 on v5

--- a/solution.py
+++ b/solution.py
@@ -319,9 +319,9 @@
     for first in range(0, 4096, DEEP):
         at = pl.ds(first, DEEP)
         stage[:, at] = (base[:, at] + dot(right[...], left[:, at], 1, 0)).astype(BF)
-        for k in range(4):
-            piece = pl.ds(first + k * 256, 256)
-            write = pltpu.make_async_copy(stage.at[:, piece], out.at[0, :, piece], sem.at[len(writes)])
+        for k in range(8):
+            piece, rows = pl.ds(first + k // 2 * 256, 256), pl.ds(k % 2 * HALF, HALF)
+            write = pltpu.make_async_copy(stage.at[rows, piece], out.at[0, rows, piece], sem.at[len(writes)])
             write.start()
             writes.append(write)
     q_out[...] = qt[...]
@@ -388,7 +388,7 @@
         out_shape=(jax.ShapeDtypeStruct(error.shape, BF), jax.ShapeDtypeStruct((rank, ff), F32)),
         in_specs=[vmem] * 4,
         out_specs=(anywhere, vmem),
-        scratch_shapes=[pltpu.VMEM((ff, dw), BF), dma((16,))],
+        scratch_shapes=[pltpu.VMEM((ff, dw), BF), dma((32,))],
         compiler_params=pltpu.CompilerParams(vmem_limit_bytes=24 * 2**20),
         name="new_error",
     )(base, left, right, qt)

time: 74.6 us -> 74.7 us (level)
  no operation moved by 1% of the time
where the time goes in v6:
time: 74.7 us; the launch traced here: 74.6 us
  Pallas kernels  74 us (99%)
    pallas_call x1, Pallas kernels, local(): pl.pallas_call(factors_kernel, out_shape=(pltpu.VMEM((4 * rank, dw), BF),...  68 us
    pallas_call x1, Pallas kernels, local(): pl.pallas_call(error_kernel, out_shape=(jax.ShapeDtypeStruct(error.shape,...  5.99 us

profile of v6, /device:TPU:1, one launch (start us, length us, event | category | flops | bytes accessed | tf_op | source)
XLA Modules:
  0.0 74.6 jit_solution(8675369941739063570)
XLA Ops:
  0.6 68.0 %power_iterations.1 = (bf16[128,4096]{1,0:T(8,128)(2,1)S(1)}, bf16[1376,128]{1,0:T(8,128)(2,1)S(1)}, f32[32,1376]{1,0:T(8,128)S(1)}, f32[1376,4096]{1,0:T(8,128)S(1)}) custom-call(bf16[384,4096]{1,0:T(8,128)(2,1)} %x_h.1, bf16[1376,384]{1,0:T(8,128)(2,1)} %bitcast.6, bf16[1,1376,4096]{2,1,0:T(8,128)(2,1)} %bitcast.5, f32[32,1376]{1,0:T(8,128)} %bitcast.7), custom_call_target="tpu_custom_call" | custom-call | tf_op jit(solution)/shard_map/power_iterations/pallas_call | solution.py:339
  68.6 6.0 %new_error.1 = (bf16[1,1376,4096]{2,1,0:T(8,128)(2,1)}, f32[32,1376]{1,0:T(8,128)}) custom-call(f32[1376,4096]{1,0:T(8,128)S(1)} %get-tuple-element.8.base, bf16[128,4096]{1,0:T(8,128)(2,1)S(1)} %get-tuple-element.9.left, bf16[1376,128]{1,0:T(8,128)(2,1)S(1)} %get-tuple-element.10.right, f32[32,1376]{1,0:T(8,128)S(1)} %get-tuple-element.11.qt), custom_call_target="tpu_custom_call" | custom-call | tf_op jit(solution)/shard_map/new_error/pallas_call | solution.py:386
